TPU v7x, 32 devices: a whole 2x2x4 slice. The times are simulated.
32 devices in a mesh: days: 2 (over x), sta: 16 (over z, y, core).
Axes of the slice: x: 2, y: 2, z: 4, core: 2. Of those that a mesh axis runs over, the one named last changes fastest.
Arguments:
- records: bfloat16 [384, 256, 256], P(('days', 'sta')), parts along dimension 0, may hold values from -330 to 330
- counts: int32 [128, 4], P(('days', 'sta')), parts along dimension 0, may hold values from 0 to 64
- gap_mask: int32 [128, 256], P(('days', 'sta')), parts along dimension 0, may hold values 0 or 1
Outputs:
- cross_spectra: bfloat16 [7, 2, 384, 12, 128], P(None, None, ('days', 'sta')), parts along dimension 2
There are 2 independent parts, one for each index of `days`. A program takes and returns all parts, laid end to end along the dimension named above; each array names one. Nothing has to cross between parts.
All inputs are finite; a program needn't handle non-finite values. No bound on the sum of `gap_mask` on one device may be relied on, other than what follows from the above.
Results may differ from a plain program's by a relative error of at most 0.0062.
Values may be sent and summed in bfloat16 or wider, within the bound.
A program may use at most 64 MiB of HBM per device.

v0:
```python
import math

import jax
import jax.numpy as jnp
from jax import lax
from jax.sharding import PartitionSpec as P

ROUNDS = 3


epsilon = 1e-06


def from_behind(value, axis, steps):
    count = lax.axis_size(axis)
    pairs = [(source, (source + steps) % count) for source in range(count)]
    return lax.ppermute(value, axis, pairs)


def fourier_matrix(samples):
    freq_bins = samples // 2
    times_axis = jnp.arange(samples, dtype=jnp.int32)
    bins_axis = jnp.arange(freq_bins, dtype=jnp.int32)
    phase_idx = times_axis[:, None] * bins_axis[None, :] % samples
    angle = 2.0 * math.pi / samples * phase_idx.astype(jnp.float32)
    taper = 0.5 - 0.5 * jnp.cos(2.0 * math.pi / samples * (times_axis.astype(jnp.float32) + 0.5))
    table_full = jnp.concatenate(
        [taper[:, None] * jnp.cos(angle), -taper[:, None] * jnp.sin(angle)], axis=1
    )
    return table_full.astype(jnp.bfloat16)


def whiten(records, counts, gap_mask, fourier):
    channels, segments, samples = records.shape
    stations, hour_count = counts.shape
    seg_hour = segments // hour_count
    spectrum = jnp.dot(
        records.reshape(channels * segments, samples), fourier, preferred_element_type=jnp.float32
    ).reshape(channels, segments, samples)
    band_power = jnp.mean(spectrum * spectrum, axis=2, keepdims=True)
    position = jnp.arange(seg_hour, dtype=jnp.int32)
    station_valid = (position[None, None, :] < counts[:, :, None]).astype(jnp.float32)
    station_valid = station_valid * gap_mask.reshape(stations, hour_count, seg_hour).astype(
        jnp.float32
    )
    validity = jnp.repeat(station_valid.reshape(stations, segments), 3, axis=0)
    whitened = (spectrum * lax.rsqrt(band_power + epsilon) * validity[:, :, None]).astype(
        jnp.bfloat16
    )
    return (
        whitened.reshape(channels, hour_count, seg_hour, 2, samples // 2),
        validity.astype(jnp.bfloat16).reshape(channels, hour_count, seg_hour),
    )


def pair_spectra(own_block, partner, own_valid, partner_valid):
    channels = own_block.shape[0]
    hour_count = own_block.shape[1]
    turned = jnp.stack([own_block[:, :, :, 1], -own_block[:, :, :, 0]], axis=3)
    stacked = jnp.concatenate([own_block, turned], axis=0)
    products = jnp.einsum("xhspk,bhspk->hkxb", stacked, partner, preferred_element_type=jnp.float32)
    joint = jnp.einsum("ahs,bhs->hab", own_valid, partner_valid, preferred_element_type=jnp.float32)
    weighting = 1.0 / (hour_count * jnp.maximum(joint, 1.0))
    weighting = jnp.concatenate([weighting, weighting], axis=1)
    summed = jnp.sum(products * weighting[:, None], axis=0)
    summed = summed.reshape(summed.shape[0], 2, channels, channels)
    return jnp.transpose(summed, (1, 2, 3, 0)).astype(jnp.bfloat16)


def fetch_partner(whitened, validity, offset):
    return from_behind((whitened, validity), "sta", offset)


def per_device(records, counts, gap_mask):
    fourier = fourier_matrix(records.shape[2])
    whitened, validity = whiten(records, counts, gap_mask, fourier)
    blocks = [None] * (2 * ROUNDS + 1)
    blocks[ROUNDS] = pair_spectra(whitened, whitened, validity, validity)
    lower_pair = (whitened, validity)
    for distance in range(1, ROUNDS + 1):
        lower_pair = fetch_partner(whitened, validity, distance)
        blocks[ROUNDS - distance] = pair_spectra(whitened, lower_pair[0], validity, lower_pair[1])
        returned = from_behind(blocks[ROUNDS - distance], "sta", -distance)
        blocks[ROUNDS + distance] = jnp.stack(
            [jnp.transpose(returned[0], (1, 0, 2)), -jnp.transpose(returned[1], (1, 0, 2))]
        )
    return jnp.stack(blocks)


def solution(mesh):
    in_specs = (P(("days", "sta"), None, None), P(("days", "sta"), None), P(("days", "sta"), None))
    out_specs = P(None, None, ("days", "sta"), None, None)
    return jax.shard_map(
        per_device, mesh=mesh, in_specs=in_specs, out_specs=out_specs, check_vma=False
    )
```

profile of v0, /device:TPU:0, one launch (start us, length us, event | category | flops | bytes accessed | tf_op | source)
XLA Modules:
  0.0 168.8 jit_solution(1466548831174266084)
XLA Ops:
  0.1 0.6 multiply_convert_fusion
  0.7 0.8 copy-done
  1.4 2.3 %multiply_reduce_fusion = (f32[3072]{0:T(1024)S(1)}, f32[3072,256]{0,1:T(8,128)}) fusion(bf16[3072,256]{1,0:T(8,128)(2,1)S(1)} %bitcast.112, bf16[256,128]{1,0:T(8,128)(2,1)S(1)} %get-tuple-element.19, bf16[256,128]{1,0:T(8,128)(2,1)S(1)} %get-tuple-element.20), kind=kOutput, calls=%fused_computation.13 | convolution fusion | flops 404485120 | bytes 4861952 | tf_op jit(solution)/shard_map/dot_general | solution.py:37
  3.7 7.3 %reshape.72 = f32[12,4,64,2,128]{2,1,0,4,3:T(4,128)} reshape(f32[3072,256]{0,1:T(8,128)} %get-tuple-element.18) | data formatting | bytes 6291456 | tf_op jit(solution)/shard_map/reshape | solution.py:39
  11.0 0.1 rsqrt.12
  11.1 0.1 lt.32
  11.2 0.1 lt.33
  11.3 0.1 lt.30
  11.4 0.1 mul.157
  11.5 5.8 %fusion.1 = bf16[12,4,64,2,128]{2,0,3,4,1:T(8,128)(2,1)} fusion(f32[12,4,64,2,128]{2,1,0,4,3:T(4,128)} %reshape.72, f32[12,4,64]{2,0,1:T(8,128)S(1)} %copy.87, f32[12,4,64]{2,0,1:T(8,128)S(1)} %copy.85), kind=kLoop, calls=%fused_computation.2 | loop fusion | flops 2359296 | bytes 4743168 | tf_op jit(solution)/shard_map/convert_element_type | solution.py:47
  17.3 5.9 %copy.88 = bf16[12,4,64,2,128]{4,2,3,1,0:T(8,128)(2,1)} copy(bf16[12,4,64,2,128]{2,0,3,4,1:T(8,128)(2,1)} %fusion.1) | data formatting | bytes 3145728 | tf_op jit(solution)/shard_map/convert_element_type | solution.py:47
  23.1 3.0 %collective-permute-start.2 = (bf16[12,4,64,2,128]{4,2,3,1,0:T(8,128)(2,1)}, bf16[12,4,64,2,128]{4,2,3,1,0:T(8,128)(2,1)}, u32[]{:S(2)}, u32[]{:S(2)}) collective-permute-start(bf16[12,4,64,2,128]{4,2,3,1,0:T(8,128)(2,1)} %copy.88), channel_id=1, source_target_pairs={{0,2},{1,3},{2,4},{3,5},{4,6},{5,7},{6,8},{7,9},{8,10},{9,11},{10,... | collective-permute-start | bytes 4718600 | tf_op jit(solution)/shard_map/ppermute | solution.py:17
  26.1 0.7 collective-permute-start
  26.8 1.5 collective-permute-start.3
  28.3 1.9 %collective-permute-start.1 = (bf16[12,4,64]{2,0,1:T(8,128)(2,1)S(1)}, bf16[12,4,64]{2,0,1:T(8,128)(2,1)S(1)}, u32[]{:S(2)}, u32[]{:S(2)}) collective-permute-start(bf16[12,4,64]{2,0,1:T(8,128)(2,1)S(1)} %copy.129), channel_id=1, source_target_pairs={{0,3},{1,4},{2,5},{3,6},{4,7},{5,8},{6,9},{7,10},{8,11},{9,12},{10... | collective-permute-start | bytes 18440 | tf_op jit(solution)/shard_map/ppermute | solution.py:17
  30.2 4.6 %fusion.31 = (bf16[12,4,64,1,128]{2,0,3,4,1:T(8,128)(2,1)}, bf16[12,4,64,1,128]{2,0,3,4,1:T(8,128)(2,1)}) fusion(bf16[12,4,64,2,128]{2,0,3,4,1:T(8,128)(2,1)} %fusion.1), kind=kLoop, calls=%fused_computation.74 | loop fusion | flops 393216 | bytes 3145728 | tf_op jit(solution)/shard_map/slice | solution.py:59
  34.8 0.1 fusion.7
  34.9 0.1 pad_maximum_fusion.3
  35.0 5.0 %fusion.2 = bf16[128,24,12]{1,2,0:T(8,128)(2,1)S(1)} fusion(bf16[12,4,64,2,128]{2,0,3,4,1:T(8,128)(2,1)S(1)} %copy-done.1, f32[4,24,12]{1,2,0:T(8,128)S(1)} %pad_maximum_fusion.3, bf16[12,4,64,1,128]{2,0,3,4,1:T(8,128)(2,1)} %get-tuple-element.6, bf16[12,4,64,1,128]{2,0,3,4,1:T(8,128)(2,1)} %get-tuple-element.5), kind=kOutput, calls=%fused_computation.5 | convolution fusion | flops 47443968 | bytes 3224064 | tf_op jit(solution)/shard_map/xhspk,bhspk->hkxb/dot_general | solution.py:61
  40.0 0.4 copy.101
  40.4 58.2 %collective-permute-done.3 = bf16[12,4,64]{2,0,1:T(8,128)(2,1)S(1)} collective-permute-done((bf16[12,4,64]{2,0,1:T(8,128)(2,1)S(1)}, bf16[12,4,64]{2,0,1:T(8,128)(2,1)S(1)}, u32[]{:S(2)}, u32[]{:S(2)}) %collective-permute-start.3) | collective-permute-done | bytes 6176 | tf_op jit(solution)/shard_map/ppermute | solution.py:17
  98.6 0.0 collective-permute-start.5
  98.6 0.1 fusion.11
  98.8 0.0 collective-permute-done.1
  98.8 0.1 fusion.13
  98.9 0.1 pad_maximum_fusion.1
  99.0 0.1 pad_maximum_fusion
  99.1 16.1 %collective-permute-done.5 = bf16[12,4,64]{2,0,1:T(8,128)(2,1)S(1)} collective-permute-done((bf16[12,4,64]{2,0,1:T(8,128)(2,1)S(1)}, bf16[12,4,64]{2,0,1:T(8,128)(2,1)S(1)}, u32[]{:S(2)}, u32[]{:S(2)}) %collective-permute-start.5) | collective-permute-done | bytes 6176 | tf_op jit(solution)/shard_map/ppermute | solution.py:17
  115.2 0.1 fusion.9
  115.3 0.1 pad_maximum_fusion.2
  115.4 7.4 %copy.94 = bf16[12,4,64,2,128]{2,0,3,4,1:T(8,128)(2,1)} copy(bf16[12,4,64,2,128]{4,2,3,1,0:T(8,128)(2,1)} %collective-permute-done.2) | data formatting | bytes 3145728 | tf_op jit(solution)/shard_map/ppermute | solution.py:17
  122.8 7.4 %fusion.4 = bf16[128,24,12]{1,2,0:T(8,128)(2,1)S(1)} fusion(bf16[12,4,64,2,128]{2,0,3,4,1:T(8,128)(2,1)} %copy.94, f32[4,24,12]{1,2,0:T(8,128)S(1)} %pad_maximum_fusion.1, bf16[12,4,64,1,128]{2,0,3,4,1:T(8,128)(2,1)} %get-tuple-element.6, bf16[12,4,64,1,128]{2,0,3,4,1:T(8,128)(2,1)} %get-tuple-element.5, bf16[12,4,64,2,128]{2,0,3,4,1:T(8,128)(2,1)} %fusion.1), kind=kOutput, calls=%fused_computation.9 | convolution fusion | flops 47443968 | bytes 4796928 | tf_op jit(solution)/shard_map/xhspk,bhspk->hkxb/dot_general | solution.py:61
  130.2 0.4 copy.95
  130.6 0.0 collective-permute-done
  130.6 7.4 %copy.89 = bf16[12,4,64,2,128]{2,0,3,4,1:T(8,128)(2,1)} copy(bf16[12,4,64,2,128]{4,2,3,1,0:T(8,128)(2,1)} %collective-permute-done) | data formatting | bytes 3145728 | tf_op jit(solution)/shard_map/ppermute | solution.py:17
  138.0 7.4 %fusion.5 = bf16[128,24,12]{1,2,0:T(8,128)(2,1)S(1)} fusion(bf16[12,4,64,2,128]{2,0,3,4,1:T(8,128)(2,1)} %copy.89, f32[4,24,12]{1,2,0:T(8,128)S(1)} %pad_maximum_fusion, bf16[12,4,64,1,128]{2,0,3,4,1:T(8,128)(2,1)} %get-tuple-element.6, bf16[12,4,64,1,128]{2,0,3,4,1:T(8,128)(2,1)} %get-tuple-element.5, bf16[12,4,64,2,128]{2,0,3,4,1:T(8,128)(2,1)} %fusion.1), kind=kOutput, calls=%fused_computation.11 | convolution fusion | flops 47443968 | bytes 4796928 | tf_op jit(solution)/shard_map/xhspk,bhspk->hkxb/dot_general | solution.py:61
  145.4 0.4 copy.91
  145.9 0.0 collective-permute-done.4
  145.9 7.4 %copy.98 = bf16[12,4,64,2,128]{2,0,3,4,1:T(8,128)(2,1)} copy(bf16[12,4,64,2,128]{4,2,3,1,0:T(8,128)(2,1)} %collective-permute-done.4) | data formatting | bytes 3145728 | tf_op jit(solution)/shard_map/ppermute | solution.py:17
  153.3 7.4 %fusion.3 = bf16[128,24,12]{1,2,0:T(8,128)(2,1)S(1)} fusion(bf16[12,4,64,2,128]{2,0,3,4,1:T(8,128)(2,1)} %copy.98, f32[4,24,12]{1,2,0:T(8,128)S(1)} %pad_maximum_fusion.2, bf16[12,4,64,1,128]{2,0,3,4,1:T(8,128)(2,1)} %get-tuple-element.6, bf16[12,4,64,1,128]{2,0,3,4,1:T(8,128)(2,1)} %get-tuple-element.5, bf16[12,4,64,2,128]{2,0,3,4,1:T(8,128)(2,1)} %fusion.1), kind=kOutput, calls=%fused_computation.7 | convolution fusion | flops 47443968 | bytes 4796928 | tf_op jit(solution)/shard_map/xhspk,bhspk->hkxb/dot_general | solution.py:61
  160.7 0.4 copy.99
  161.1 0.1 collective-permute-start.6
  161.2 0.1 collective-permute-start.7
  161.2 1.7 %collective-permute-start.8 = (bf16[2,12,12,128]{3,1,0,2:T(8,128)(2,1)S(1)}, bf16[2,12,12,128]{3,1,0,2:T(8,128)(2,1)S(1)}, u32[]{:S(2)}, u32[]{:S(2)}) collective-permute-start(bf16[2,12,12,128]{3,1,0,2:T(8,128)(2,1)S(1)} %bitcast.119), channel_id=1, source_target_pairs={{0,13},{1,14},{2,15},{3,0},{4,1},{5,2},{6,3},{7,4},{8,5},{9,6},{10... | collective-permute-start | bytes 221192 | tf_op jit(solution)/shard_map/ppermute | solution.py:17
  163.1 1.1 collective-permute-done.6
  164.2 2.6 %collective-permute-done.7 = bf16[2,12,12,128]{3,1,2,0:T(8,128)(2,1)S(1)} collective-permute-done((bf16[2,12,12,128]{3,1,2,0:T(8,128)(2,1)S(1)}, bf16[2,12,12,128]{3,1,2,0:T(8,128)(2,1)S(1)}, u32[]{:S(2)}, u32[]{:S(2)}) %collective-permute-start.7) | collective-permute-done | bytes 73760 | tf_op jit(solution)/shard_map/ppermute | solution.py:17
  166.9 0.6 collective-permute-done.8
  167.5 1.3 copy.106
  (34 shorter events, 0.5 us)
Async XLA Ops:
  0.0 1.4 copy-start
  3.7 7.4 %copy-start.3 = (s32[4,4]{1,0:T(4,128)S(1)}, s32[4,4]{1,0:T(4,128)}, u32[]{:S(2)}) copy-start(s32[4,4]{1,0:T(4,128)} %param.4) | copy-start | bytes 196
  3.7 7.6 %copy-start.2 = (s32[4,256]{1,0:T(4,128)S(1)}, s32[4,256]{1,0:T(4,128)}, u32[]{:S(2)}) copy-start(s32[4,256]{1,0:T(4,128)} %param.5) | copy-start | bytes 12292
  23.1 92.3 %collective-permute-start.2 = (bf16[12,4,64,2,128]{4,2,3,1,0:T(8,128)(2,1)}, bf16[12,4,64,2,128]{4,2,3,1,0:T(8,128)(2,1)}, u32[]{:S(2)}, u32[]{:S(2)}) collective-permute-start(bf16[12,4,64,2,128]{4,2,3,1,0:T(8,128)(2,1)} %copy.88), channel_id=1, source_target_pairs={{0,2},{1,3},{2,4},{3,5},{4,6},{5,7},{6,8},{7,9},{8,10},{9,11},{10,... | collective-permute-start | bytes 4718600 | tf_op jit(solution)/shard_map/ppermute | solution.py:17
  26.1 104.5 %collective-permute-start = (bf16[12,4,64,2,128]{4,2,3,1,0:T(8,128)(2,1)}, bf16[12,4,64,2,128]{4,2,3,1,0:T(8,128)(2,1)}, u32[]{:S(2)}, u32[]{:S(2)}) collective-permute-start(bf16[12,4,64,2,128]{4,2,3,1,0:T(8,128)(2,1)} %copy.88), channel_id=1, source_target_pairs={{0,3},{1,4},{2,5},{3,6},{4,7},{5,8},{6,9},{7,10},{8,11},{9,12},{10... | collective-permute-start | bytes 4718600 | tf_op jit(solution)/shard_map/ppermute | solution.py:17
  26.8 8.2 %copy-start.1 = (bf16[12,4,64,2,128]{2,0,3,4,1:T(8,128)(2,1)S(1)}, bf16[12,4,64,2,128]{2,0,3,4,1:T(8,128)(2,1)}, u32[]{:S(2)}) copy-start(bf16[12,4,64,2,128]{2,0,3,4,1:T(8,128)(2,1)} %fusion.1) | copy-start | bytes 4718596
  26.8 71.8 %collective-permute-start.3 = (bf16[12,4,64]{2,0,1:T(8,128)(2,1)S(1)}, bf16[12,4,64]{2,0,1:T(8,128)(2,1)S(1)}, u32[]{:S(2)}, u32[]{:S(2)}) collective-permute-start(bf16[12,4,64]{2,0,1:T(8,128)(2,1)S(1)} %copy.129), channel_id=1, source_target_pairs={{0,2},{1,3},{2,4},{3,5},{4,6},{5,7},{6,8},{7,9},{8,10},{9,11},{10,... | collective-permute-start | bytes 18440 | tf_op jit(solution)/shard_map/ppermute | solution.py:17
  28.3 70.5 %collective-permute-start.1 = (bf16[12,4,64]{2,0,1:T(8,128)(2,1)S(1)}, bf16[12,4,64]{2,0,1:T(8,128)(2,1)S(1)}, u32[]{:S(2)}, u32[]{:S(2)}) collective-permute-start(bf16[12,4,64]{2,0,1:T(8,128)(2,1)S(1)} %copy.129), channel_id=1, source_target_pairs={{0,3},{1,4},{2,5},{3,6},{4,7},{5,8},{6,9},{7,10},{8,11},{9,12},{10... | collective-permute-start | bytes 18440 | tf_op jit(solution)/shard_map/ppermute | solution.py:17
  30.2 115.7 %collective-permute-start.4 = (bf16[12,4,64,2,128]{4,2,3,1,0:T(8,128)(2,1)}, bf16[12,4,64,2,128]{4,2,3,1,0:T(8,128)(2,1)}, u32[]{:S(2)}, u32[]{:S(2)}) collective-permute-start(bf16[12,4,64,2,128]{4,2,3,1,0:T(8,128)(2,1)} %copy.88), channel_id=1, source_target_pairs={{0,1},{1,2},{2,3},{3,4},{4,5},{5,6},{6,7},{7,8},{8,9},{9,10},{10,1... | collective-permute-start | bytes 4718600 | tf_op jit(solution)/shard_map/ppermute | solution.py:17
  98.6 16.6 %collective-permute-start.5 = (bf16[12,4,64]{2,0,1:T(8,128)(2,1)S(1)}, bf16[12,4,64]{2,0,1:T(8,128)(2,1)S(1)}, u32[]{:S(2)}, u32[]{:S(2)}) collective-permute-start(bf16[12,4,64]{2,0,1:T(8,128)(2,1)S(1)} %copy.129), channel_id=1, source_target_pairs={{0,1},{1,2},{2,3},{3,4},{4,5},{5,6},{6,7},{7,8},{8,9},{9,10},{10,1... | collective-permute-start | bytes 18440 | tf_op jit(solution)/shard_map/ppermute | solution.py:17
  161.1 3.1 %collective-permute-start.6 = (bf16[2,12,12,128]{3,1,2,0:T(8,128)(2,1)S(1)}, bf16[2,12,12,128]{3,1,2,0:T(8,128)(2,1)S(1)}, u32[]{:S(2)}, u32[]{:S(2)}) collective-permute-start(bf16[2,12,12,128]{3,1,2,0:T(8,128)(2,1)S(1)} %bitcast.115), channel_id=1, source_target_pairs={{0,15},{1,0},{2,1},{3,2},{4,3},{5,4},{6,5},{7,6},{8,7},{9,8},{10,9... | collective-permute-start | bytes 221192 | tf_op jit(solution)/shard_map/ppermute | solution.py:17
  161.2 5.6 %collective-permute-start.7 = (bf16[2,12,12,128]{3,1,2,0:T(8,128)(2,1)S(1)}, bf16[2,12,12,128]{3,1,2,0:T(8,128)(2,1)S(1)}, u32[]{:S(2)}, u32[]{:S(2)}) collective-permute-start(bf16[2,12,12,128]{3,1,2,0:T(8,128)(2,1)S(1)} %bitcast.113), channel_id=1, source_target_pairs={{0,14},{1,15},{2,0},{3,1},{4,2},{5,3},{6,4},{7,5},{8,6},{9,7},{10,... | collective-permute-start | bytes 221192 | tf_op jit(solution)/shard_map/ppermute | solution.py:17
  161.2 6.2 %collective-permute-start.8 = (bf16[2,12,12,128]{3,1,0,2:T(8,128)(2,1)S(1)}, bf16[2,12,12,128]{3,1,0,2:T(8,128)(2,1)S(1)}, u32[]{:S(2)}, u32[]{:S(2)}) collective-permute-start(bf16[2,12,12,128]{3,1,0,2:T(8,128)(2,1)S(1)} %bitcast.119), channel_id=1, source_target_pairs={{0,13},{1,14},{2,15},{3,0},{4,1},{5,2},{6,3},{7,4},{8,5},{9,6},{10... | collective-permute-start | bytes 221192 | tf_op jit(solution)/shard_map/ppermute | solution.py:17
where the time goes:
time: 169 us
  waiting for transfers between devices  78.6 us (47%)
  local copies, waits for them, and re-layouts  39.5 us (23%)
  matrix products  30.1 us (18%)
  other arithmetic  11.5 us (7%)
  starting transfers between devices  8.87 us (5%)
    ppermute x9, waiting for transfers between devices, from_behind(): return lax.ppermute(value, axis, pairs)  78.6 us
    dot_general x4, matrix products, pair_spectra(): jnp.einsum('xhspk,bhspk->hkxb', stacked, partner, preferred_element_type=...  27.2 us
    ppermute x3, local copies, waits for them, and re-layouts, from_behind(): return lax.ppermute(value, axis, pairs)  22.2 us
    ppermute x9, starting transfers between devices, from_behind(): return lax.ppermute(value, axis, pairs)  8.87 us
    reshape x1, local copies, waits for them, and re-layouts, whiten(): spectrum = jnp.dot(records.reshape(channels * segments, samples), fourier...  7.26 us
    convert_element_type x1, local copies, waits for them, and re-layouts, whiten(): (spectrum * lax.rsqrt(band_power + epsilon) * validity[:, :, None]).astyp...  5.86 us
    convert_element_type x1, other arithmetic, whiten(): (spectrum * lax.rsqrt(band_power + epsilon) * validity[:, :, None]).astyp...  5.81 us
    slice x1, other arithmetic, pair_spectra(): turned = jnp.stack([own_block[:, :, :, 1], -own_block[:, :, :, 0]], axis=3)  4.62 us
  transfers between devices with their start and end apart: 9, of which 5 were waited for; matrix products, arithmetic and copies ran while one was open for 25% of the time, Pallas kernels for 0%

commit v1 on v0

v1 whole, which is shorter than its diff:
```python
import functools

import jax
import jax.numpy as jnp
import numpy as np
from jax import lax
from jax.experimental import pallas as pl
from jax.experimental.pallas import tpu as pltpu
from jax.sharding import PartitionSpec as P

ROUNDS = 3
TILE = 16
LANES = 128
EPSILON = 1e-06
NT = (((1,), (1,)), ((), ()))


def fourier_rows(samples):
    bins = samples // 2
    times = np.arange(samples, dtype=np.int32)
    phase = (times[:, None] * np.arange(bins, dtype=np.int32)[None, :]) % samples
    angle = np.float32(2.0 * np.pi / samples) * phase.astype(np.float32)
    half = times.astype(np.float32) + np.float32(0.5)
    taper = np.float32(0.5) - np.float32(0.5) * np.cos(np.float32(2.0 * np.pi / samples) * half)
    table = np.concatenate([taper[:, None] * np.cos(angle), -taper[:, None] * np.sin(angle)], axis=1)
    return jnp.asarray(np.ascontiguousarray(table.T), dtype=jnp.bfloat16)


def pick_rows(channels):
    out = np.zeros((2 * TILE, 2 * channels * TILE), np.float32)
    for part in range(2):
        for a in range(channels):
            start = (part * channels + a) * TILE
            out[part * TILE + a, start : start + TILE] = 1
    return jnp.asarray(out, dtype=jnp.bfloat16)


def spread_bins(channels, bins):
    row = np.arange(channels * TILE)
    col = np.arange(channels * bins)
    same = (row[:, None] // TILE == col[None, :] // bins) & (row[:, None] % TILE == col[None, :] % TILE)
    return jnp.asarray(same.astype(np.float32), dtype=jnp.bfloat16)


def kernel(
    dims, table, pick, spread, records, counts, gaps, lower, upper,
    own, turned, inbox, weights, gathered, outgoing, returned,
    send_sem, recv_sem, back_send, back_recv,
):
    channels, segments, samples, stations, hours, count = dims
    bins = samples // 2
    span = segments // hours
    groups = bins // TILE
    rows = channels * TILE
    per_station = channels // stations
    me = lax.axis_index("sta")
    kind = lax.rem(me, 4)
    core = lax.rem(kind, 2)
    side = kind // 2

    def at(offset):
        return lax.rem(me + offset + count, count)

    def barrier_signal():
        barrier = pltpu.get_barrier_semaphore()
        for offset in (1, 2, 3, 4, -1, -2, -3, -4):
            pl.semaphore_signal(
                barrier, inc=1, device_id={"sta": at(offset)}, device_id_type=pl.DeviceIdType.MESH
            )

    barrier_signal()

    position = lax.broadcasted_iota(jnp.int32, (stations, segments), 1)
    limit = jnp.zeros((stations, segments), jnp.int32)
    for h in range(hours):
        limit = jnp.where(position // span == h, counts[:, h : h + 1], limit)
    valid = jnp.where(lax.rem(position, span) < limit, gaps[...], 0).astype(jnp.float32)
    valid = jnp.concatenate(
        [jnp.broadcast_to(valid[s : s + 1], (per_station, segments)) for s in range(stations)]
        + [jnp.zeros((TILE - channels, segments), jnp.float32)],
        axis=0,
    )
    left = lax.broadcasted_iota(jnp.int32, (TILE, LANES), 1) < span
    for pair in range(hours // 2):
        block = valid[:, pair * LANES : (pair + 1) * LANES]
        first = jnp.where(left, block, 0.0)
        second = jnp.where(left, pltpu.roll(block, span, 1), 0.0)
        own[0, :, 2 * pair * LANES : (2 * pair + 1) * LANES] = first.astype(jnp.bfloat16)
        own[0, :, (2 * pair + 1) * LANES : (2 * pair + 2) * LANES] = second.astype(jnp.bfloat16)

    left_b = lax.broadcasted_iota(jnp.int32, (bins, LANES), 1) < span
    for c in range(channels):
        spectrum = lax.dot_general(table[...], records[c], NT, preferred_element_type=jnp.float32)
        power = jnp.sum(spectrum * spectrum, axis=0, keepdims=True) * (1.0 / samples)
        white = spectrum * (lax.rsqrt(power + EPSILON) * valid[c : c + 1])
        for pair in range(hours // 2):
            re = white[:bins, pair * LANES : (pair + 1) * LANES]
            im = white[bins:, pair * LANES : (pair + 1) * LANES]
            re_r = pltpu.roll(re, span, 1)
            im_r = pltpu.roll(im, span, 1)
            straight = (jnp.where(left_b, re, im_r), jnp.where(left_b, re_r, im))
            across = (jnp.where(left_b, im, -re_r), jnp.where(left_b, im_r, -re))
            for half in range(2):
                lanes = slice((2 * pair + half) * LANES, (2 * pair + half + 1) * LANES)
                flat = straight[half].astype(jnp.bfloat16)
                flat_t = across[half].astype(jnp.bfloat16)
                for g in range(groups):
                    own[1 + g * channels + c, :, lanes] = flat[g * TILE : (g + 1) * TILE]
                    turned[g * channels + c, :, lanes] = flat_t[g * TILE : (g + 1) * TILE]

    pl.semaphore_wait(pltpu.get_barrier_semaphore(), 8)

    def where_is(piece):
        if isinstance(piece, int) and piece == 0:
            return pl.ds(0, 1)
        return pl.ds(1 + (piece - 1) * channels, channels)

    def copy(source, piece, way, slot, target):
        return pltpu.make_async_remote_copy(
            src_ref=source.at[where_is(piece)],
            dst_ref=inbox.at[slot, where_is(piece)],
            send_sem=send_sem.at[way, piece],
            recv_sem=recv_sem.at[slot, piece],
            device_id={"sta": target},
            device_id_type=pl.DeviceIdType.MESH,
        )

    def ahead(piece):
        return copy(own, piece, 0, 1 + 2 * side, at(2 + 2 * side))

    def beside(piece):
        return copy(own, piece, 1, 2 * core, at(1 + 2 * core))

    def relay_twin(piece):
        return copy(inbox.at[1], piece, 2, 2 - 2 * core, at(1 - 2 * core))

    def relay_down(piece):
        return copy(inbox.at[3], piece, 3, 1, at(-2))

    def relay_twin_far(piece):
        return copy(inbox.at[3], piece, 1, 2, at(-1))

    def arrived(slot, piece):
        copy(own, piece, 0, slot, at(1)).wait_recv()

    def send_own(piece):
        ahead(piece).start()

        @pl.when(kind != 3)
        def _():
            beside(piece).start()

    def pass_on(piece):
        @pl.when(side == 1)
        def _():
            arrived(3, piece)
            relay_down(piece).start()

        @pl.when(kind == 3)
        def _():
            relay_twin_far(piece).start()

        arrived(1, piece)
        relay_twin(piece).start()

    send_own(0)
    for g in range(groups):
        send_own(1 + g)

    def dot_nt(a, b):
        return lax.dot_general(a, b, NT, preferred_element_type=jnp.float32)

    row_id = lax.broadcasted_iota(jnp.int32, (rows, rows), 0)
    col_id = lax.broadcasted_iota(jnp.int32, (rows, rows), 1)
    diagonal = lax.rem(row_id, TILE) == lax.rem(col_id, TILE)

    def widen(ref, h):
        block = ref[0, :, h * LANES : (h + 1) * LANES].astype(jnp.float32)
        return jnp.concatenate(
            [jnp.broadcast_to(block[c : c + 1], (TILE, LANES)) for c in range(channels)], axis=0
        ).astype(jnp.bfloat16)

    def weigh(d, partner):
        for h in range(hours):
            joint = dot_nt(widen(own, h), widen(partner, h))
            weights[d, h] = jnp.where(diagonal, 1.0 / (hours * jnp.maximum(joint, 1.0)), 0.0)

    lane_group = lax.rem(lax.broadcasted_iota(jnp.int32, (2 * TILE, channels * bins), 1), bins) // TILE

    def correlate(d, partner, g):
        at_rows = pl.ds(1 + g * channels, channels)
        t_rows = pl.ds(g * channels, channels)
        re = jnp.zeros((rows, rows), jnp.float32)
        im = jnp.zeros((rows, rows), jnp.float32)
        for h in range(hours):
            lanes = slice(h * LANES, (h + 1) * LANES)
            other = partner[at_rows, :, lanes].reshape(rows, LANES)
            mine = own[at_rows, :, lanes].reshape(rows, LANES)
            mine_t = turned[t_rows, :, lanes].reshape(rows, LANES)
            scale = weights[d, h]
            re = re + dot_nt(mine, other) * scale
            im = im + dot_nt(mine_t, other) * scale
        both = jnp.concatenate([re, im], axis=0).astype(jnp.bfloat16)
        picked = jnp.dot(pick[...], both, preferred_element_type=jnp.float32).astype(jnp.bfloat16)
        wide = jnp.dot(picked, spread[...], preferred_element_type=jnp.float32)
        gathered[d] = jnp.where(lane_group == g, wide, gathered[d])

    gathered[...] = jnp.zeros_like(gathered)
    weigh(0, own)

    @pl.loop(0, groups)
    def _(g):
        correlate(0, own, g)

    pass_on(0)
    arrived(0, 0)
    arrived(2, 0)
    for d in range(1, ROUNDS + 1):
        weigh(d, inbox.at[d - 1])

    @pl.loop(0, groups)
    def _(g):
        pass_on(g + 1)
        arrived(0, g + 1)
        arrived(2, g + 1)
        for d in range(1, ROUNDS + 1):
            correlate(d, inbox.at[d - 1], g)

    def give_back(d):
        return pltpu.make_async_remote_copy(
            src_ref=outgoing.at[d - 1],
            dst_ref=returned.at[d - 1],
            send_sem=back_send.at[d - 1],
            recv_sem=back_recv.at[d - 1],
            device_id={"sta": at(-d)},
            device_id_type=pl.DeviceIdType.MESH,
        )

    for d in range(ROUNDS, 0, -1):
        for part in range(2):
            for b in range(channels):
                value = gathered[d, part * TILE : (part + 1) * TILE, b * bins : (b + 1) * bins]
                outgoing[d - 1, part, b] = (value if part == 0 else -value).astype(jnp.bfloat16)
        give_back(d).start()
    for d in range(ROUNDS + 1):
        for part in range(2):
            for b in range(channels):
                value = gathered[d, part * TILE : (part + 1) * TILE, b * bins : (b + 1) * bins]
                lower[ROUNDS - d, part, b] = value.astype(jnp.bfloat16)

    for piece in range(groups + 1):
        ahead(piece).wait_send()
        beside(piece).wait_send()
        relay_twin(piece).wait_send()

        @pl.when(side == 1)
        def _():
            relay_down(piece).wait_send()

    for d in range(ROUNDS, 0, -1):
        give_back(d).wait()
    upper[...] = returned[...]


def per_device(count, records, counts, gap_mask):
    channels, segments, samples = records.shape
    stations, hours = counts.shape
    bins = samples // 2
    groups = bins // TILE
    rows = channels * TILE
    blocks = 1 + groups * channels
    wide = hours * LANES
    dims = (channels, segments, samples, stations, hours, count)
    vmem = pl.BlockSpec(memory_space=pltpu.VMEM)
    lower, upper = pl.pallas_call(
        functools.partial(kernel, dims),
        out_shape=(
            jax.ShapeDtypeStruct((ROUNDS + 1, 2, channels, TILE, bins), jnp.bfloat16),
            jax.ShapeDtypeStruct((ROUNDS, 2, channels, TILE, bins), jnp.bfloat16),
        ),
        in_specs=[vmem] * 6,
        out_specs=(vmem, vmem),
        scratch_shapes=[
            pltpu.VMEM((blocks, TILE, wide), jnp.bfloat16),
            pltpu.VMEM((blocks - 1, TILE, wide), jnp.bfloat16),
            pltpu.VMEM((ROUNDS + 1, blocks, TILE, wide), jnp.bfloat16),
            pltpu.VMEM((ROUNDS + 1, hours, rows, rows), jnp.float32),
            pltpu.VMEM((ROUNDS + 1, 2 * TILE, channels * bins), jnp.float32),
            pltpu.VMEM((ROUNDS, 2, channels, TILE, bins), jnp.bfloat16),
            pltpu.VMEM((ROUNDS, 2, channels, TILE, bins), jnp.bfloat16),
            pltpu.SemaphoreType.DMA((4, groups + 1)),
            pltpu.SemaphoreType.DMA((4, groups + 1)),
            pltpu.SemaphoreType.DMA((ROUNDS,)),
            pltpu.SemaphoreType.DMA((ROUNDS,)),
        ],
        compiler_params=pltpu.CompilerParams(
            collective_id=0, has_side_effects=True, vmem_limit_bytes=48 * 1024 * 1024
        ),
    )(
        fourier_rows(samples), pick_rows(channels), spread_bins(channels, bins),
        records, counts, gap_mask,
    )
    below = jnp.transpose(lower[:, :, :, :channels], (0, 1, 3, 2, 4))
    return jnp.concatenate([below, upper[:, :, :, :channels]], axis=0)


def solution(mesh):
    count = mesh.shape["sta"]
    return jax.shard_map(
        functools.partial(per_device, count),
        mesh=mesh,
        in_specs=(P(("days", "sta"), None, None), P(("days", "sta"), None), P(("days", "sta"), None)),
        out_specs=P(None, None, ("days", "sta"), None, None),
        check_vma=False,
    )
```

time: 169 us -> 66.5 us (0.39)
  waiting for transfers between devices: 78.6 us -> 0 us
  Pallas kernels: 0 us -> 59.2 us
  local copies, waits for them, and re-layouts: 39.5 us -> 6.89 us
  matrix products: 30.1 us -> 0 us
  other arithmetic: 11.5 us -> 0.12 us
  starting transfers between devices: 8.87 us -> 0 us
    ppermute x9 -> x0, waiting for transfers between devices: 78.6 us -> none  [from_behind(): return lax.ppermute(value, axis, pairs)]
    pallas_call x0 -> x1, Pallas kernels: none -> 59.2 us  [per_device(): pl.pallas_call(functools.partial(kernel, dims), out_shape=(jax.ShapeDtype...]
    dot_general x9 -> x0, matrix products: 30.1 us -> none  [the longest x4 27.2 us: pair_spectra(): jnp.einsum('xhspk,bhspk->hkxb', stacked, partner, preferred_element_type=...]
    ppermute x3 -> x0, local copies, waits for them, and re-layouts: 22.2 us -> none  [from_behind(): return lax.ppermute(value, axis, pairs)]
    ppermute x9 -> x0, starting transfers between devices: 8.87 us -> none  [from_behind(): return lax.ppermute(value, axis, pairs)]
    reshape x1 -> x0, local copies, waits for them, and re-layouts: 7.26 us -> none  [whiten(): spectrum = jnp.dot(records.reshape(channels * segments, samples), fourier...]
    convert_element_type x7 -> x0, local copies, waits for them, and re-layouts: 5.95 us -> none  [the longest x1 5.86 us: whiten(): (spectrum * lax.rsqrt(band_power + epsilon) * validity[:, :, None]).astyp...]
    convert_element_type x1 -> x0, other arithmetic: 5.81 us -> none  [whiten(): (spectrum * lax.rsqrt(band_power + epsilon) * validity[:, :, None]).astyp...]
  transfers between devices with their start and end apart: 9 -> 0, of which waited for: 5 -> 0; matrix products, arithmetic and copies ran while one was open for 25% -> 0% of each run, Pallas kernels for 0% -> 0%
where the time goes in v1:
time: 66.5 us; the launch traced here: 66.2 us
  Pallas kernels  59.2 us (89%)
  local copies, waits for them, and re-layouts  6.89 us (10%)
    pallas_call x1, Pallas kernels, per_device(): pl.pallas_call(functools.partial(kernel, dims), out_shape=(jax.ShapeDtype...  59.2 us
    unnamed x12, local copies, waits for them, and re-layouts  5.48 us

profile of v1, /device:TPU:0, one launch (start us, length us, event | category | flops | bytes accessed | tf_op | source)
XLA Modules:
  0.0 66.2 jit_solution(8700095411116877483)
XLA Ops:
  0.0 0.0 copy-start
  0.0 1.4 %copy-done = bf16[12,256,256]{2,1,0:T(8,128)(2,1)S(1)} copy-done((bf16[12,256,256]{2,1,0:T(8,128)(2,1)S(1)}, bf16[12,256,256]{2,1,0:T(8,128)(2,1)}, u32[]{:S(2)}) %copy-start) | copy-done | bytes 1572888
  1.4 0.0 copy-start.1
  1.4 1.1 %copy-done.1 = bf16[192,1536]{1,0:T(8,128)(2,1)S(1)} copy-done((bf16[192,1536]{1,0:T(8,128)(2,1)S(1)}, bf16[192,1536]{1,0:T(8,128)(2,1)}, u32[]{:S(2)}) %copy-start.1) | copy-done | bytes 589848
  2.5 0.0 copy-start.2
  2.5 0.9 %copy-done.2 = bf16[256,256]{1,0:T(8,128)(2,1)S(1)} copy-done((bf16[256,256]{1,0:T(8,128)(2,1)S(1)}, bf16[256,256]{1,0:T(8,128)(2,1)}, u32[]{:S(2)}) %copy-start.2) | copy-done | bytes 131096
  3.4 0.0 copy-start.3
  3.4 0.7 %copy-done.3 = bf16[32,384]{1,0:T(8,128)(2,1)S(1)} copy-done((bf16[32,384]{1,0:T(8,128)(2,1)S(1)}, bf16[32,384]{1,0:T(8,128)(2,1)}, u32[]{:S(2)}) %copy-start.3) | copy-done | bytes 24600
  4.1 0.0 copy-start.4
  4.1 0.7 %copy-done.4 = s32[4,256]{1,0:T(4,128)S(1)} copy-done((s32[4,256]{1,0:T(4,128)S(1)}, s32[4,256]{1,0:T(4,128)}, u32[]{:S(2)}) %copy-start.4) | copy-done | bytes 4120
  4.8 0.0 copy-start.5
  4.8 0.7 %copy-done.5 = s32[4,4]{1,0:T(4,128)S(1)} copy-done((s32[4,4]{1,0:T(4,128)S(1)}, s32[4,4]{1,0:T(4,128)}, u32[]{:S(2)}) %copy-start.5) | copy-done | bytes 88
  5.5 59.2 %shard_map.64 = (bf16[4,2,12,16,128]{4,3,2,1,0:T(8,128)(2,1)S(1)}, bf16[3,2,12,16,128]{4,3,2,1,0:T(8,128)(2,1)S(1)}) custom-call(bf16[256,256]{1,0:T(8,128)(2,1)S(1)} %copy-done.2, bf16[32,384]{1,0:T(8,128)(2,1)S(1)} %copy-done.3, bf16[192,1536]{1,0:T(8,128)(2,1)S(1)} %copy-done.1, bf16[12,256,256]{2,1,0:T(8,128)(2,1)S(1)} %copy-done, s32[4,4]{1,0:T(4,128)S(1)} %copy-done.5, ...), custom_call_target="tpu_custom_call" | custom-call | tf_op jit(solution)/shard_map/pallas_call | solution.py:275
  64.7 0.1 copy.7
  64.8 0.1 pad_maximum_fusion
  64.9 1.3 %copy.8 = bf16[7,2,12,12,128]{4,1,3,2,0:T(2,128)(2,1)} copy(bf16[7,2,12,12,128]{4,2,3,1,0:T(8,128)(2,1)S(1)} %pad_maximum_fusion) | data formatting | bytes 1032192 | tf_op jit(solution)/shard_map/concatenate | solution.py:304
  (1 shorter events, 0.0 us)
Async XLA Ops:
  0.0 1.4 %copy-start = (bf16[12,256,256]{2,1,0:T(8,128)(2,1)S(1)}, bf16[12,256,256]{2,1,0:T(8,128)(2,1)}, u32[]{:S(2)}) copy-start(bf16[12,256,256]{2,1,0:T(8,128)(2,1)} %records.1) | copy-start | bytes 4718596
  1.4 1.1 %copy-start.1 = (bf16[192,1536]{1,0:T(8,128)(2,1)S(1)}, bf16[192,1536]{1,0:T(8,128)(2,1)}, u32[]{:S(2)}) copy-start(bf16[192,1536]{1,0:T(8,128)(2,1)} %constant.8.clone.spread) | copy-start | bytes 1769476
  2.5 0.9 %copy-start.2 = (bf16[256,256]{1,0:T(8,128)(2,1)S(1)}, bf16[256,256]{1,0:T(8,128)(2,1)}, u32[]{:S(2)}) copy-start(bf16[256,256]{1,0:T(8,128)(2,1)} %constant.6.clone.table) | copy-start | bytes 393220
  3.4 0.7 %copy-start.3 = (bf16[32,384]{1,0:T(8,128)(2,1)S(1)}, bf16[32,384]{1,0:T(8,128)(2,1)}, u32[]{:S(2)}) copy-start(bf16[32,384]{1,0:T(8,128)(2,1)} %constant.7.clone.pick) | copy-start | bytes 73732
  4.1 0.7 %copy-start.4 = (s32[4,256]{1,0:T(4,128)S(1)}, s32[4,256]{1,0:T(4,128)}, u32[]{:S(2)}) copy-start(s32[4,256]{1,0:T(4,128)} %gaps.1) | copy-start | bytes 12292
  4.8 0.7 %copy-start.5 = (s32[4,4]{1,0:T(4,128)S(1)}, s32[4,4]{1,0:T(4,128)}, u32[]{:S(2)}) copy-start(s32[4,4]{1,0:T(4,128)} %counts.1) | copy-start | bytes 196

commit v2 on v1

--- a/solution.py
+++ b/solution.py
@@ -11,6 +11,8 @@
 ROUNDS = 3
 TILE = 16
 LANES = 128
+PARTS = 2
+LAG = 2
 EPSILON = 1e-06
 NT = (((1,), (1,)), ((), ()))
 
@@ -43,9 +45,10 @@
 
 
 def kernel(
-    dims, table, pick, spread, records, counts, gaps, lower, upper,
+    dims, table_in, pick_in, spread_in, records_in, counts_in, gaps_in, result,
+    table, pick, spread, records, counts, gaps,
     own, turned, inbox, weights, gathered, outgoing, returned,
-    send_sem, recv_sem, back_send, back_recv,
+    load_sem, send_sem, recv_sem, back_send, back_recv,
 ):
     channels, segments, samples, stations, hours, count = dims
     bins = samples // 2
@@ -68,7 +71,27 @@
                 barrier, inc=1, device_id={"sta": at(offset)}, device_id_type=pl.DeviceIdType.MESH
             )
 
+    loads = [
+        pltpu.make_async_copy(source, target, load_sem.at[i])
+        for i, (source, target) in enumerate(
+            (
+                (table_in, table), (counts_in, counts), (gaps_in, gaps),
+                (pick_in, pick), (spread_in, spread),
+            )
+        )
+    ]
+    for load in loads:
+        load.start()
+    record_loads = [
+        pltpu.make_async_copy(records_in.at[c], records.at[c], load_sem.at[len(loads) + c])
+        for c in range(channels)
+    ]
+    for load in record_loads:
+        load.start()
     barrier_signal()
+    gathered[...] = jnp.zeros_like(gathered)
+    for load in loads:
+        load.wait()
 
     position = lax.broadcasted_iota(jnp.int32, (stations, segments), 1)
     limit = jnp.zeros((stations, segments), jnp.int32)
@@ -90,6 +113,7 @@
 
     left_b = lax.broadcasted_iota(jnp.int32, (bins, LANES), 1) < span
     for c in range(channels):
+        record_loads[c].wait()
         spectrum = lax.dot_general(table[...], records[c], NT, preferred_element_type=jnp.float32)
         power = jnp.sum(spectrum * spectrum, axis=0, keepdims=True) * (1.0 / samples)
         white = spectrum * (lax.rsqrt(power + EPSILON) * valid[c : c + 1])
@@ -110,10 +134,12 @@
 
     pl.semaphore_wait(pltpu.get_barrier_semaphore(), 8)
 
+    part_rows = channels // PARTS
+
     def where_is(piece):
         if isinstance(piece, int) and piece == 0:
             return pl.ds(0, 1)
-        return pl.ds(1 + (piece - 1) * channels, channels)
+        return pl.ds(1 + (piece - 1) * part_rows, part_rows)
 
     def copy(source, piece, way, slot, target):
         return pltpu.make_async_remote_copy(
@@ -164,8 +190,8 @@
         relay_twin(piece).start()
 
     send_own(0)
-    for g in range(groups):
-        send_own(1 + g)
+    for piece in range(groups * PARTS):
+        send_own(1 + piece)
 
     def dot_nt(a, b):
         return lax.dot_general(a, b, NT, preferred_element_type=jnp.float32)
@@ -201,17 +227,32 @@
             re = re + dot_nt(mine, other) * scale
             im = im + dot_nt(mine_t, other) * scale
         both = jnp.concatenate([re, im], axis=0).astype(jnp.bfloat16)
-        picked = jnp.dot(pick[...], both, preferred_element_type=jnp.float32).astype(jnp.bfloat16)
-        wide = jnp.dot(picked, spread[...], preferred_element_type=jnp.float32)
-        gathered[d] = jnp.where(lane_group == g, wide, gathered[d])
-
-    gathered[...] = jnp.zeros_like(gathered)
+        return jnp.dot(pick[...], both, preferred_element_type=jnp.float32).astype(jnp.bfloat16)
+
+    def give_back(d, g):
+        return pltpu.make_async_remote_copy(
+            src_ref=outgoing.at[d - 1, g],
+            dst_ref=returned.at[d - 1, g],
+            send_sem=back_send.at[d - 1, g],
+            recv_sem=back_recv.at[d - 1, g],
+            device_id={"sta": at(-d)},
+            device_id_type=pl.DeviceIdType.MESH,
+        )
+
+    def place(first, picked, g):
+        wide = jnp.dot(
+            jnp.concatenate(picked, axis=0), spread[...], preferred_element_type=jnp.float32
+        )
+        for i in range(len(picked)):
+            rows_i = wide[i * 2 * TILE : (i + 1) * 2 * TILE]
+            gathered[first + i] = jnp.where(lane_group == g, rows_i, gathered[first + i])
+
+    def take_back(g):
+        for d in range(1, ROUNDS + 1):
+            give_back(d, g).wait_recv()
+        place(ROUNDS + 1, [returned[d - 1, g] for d in range(1, ROUNDS + 1)], g)
+
     weigh(0, own)
-
-    @pl.loop(0, groups)
-    def _(g):
-        correlate(0, own, g)
-
     pass_on(0)
     arrived(0, 0)
     arrived(2, 0)
@@ -220,35 +261,42 @@
 
     @pl.loop(0, groups)
     def _(g):
-        pass_on(g + 1)
-        arrived(0, g + 1)
-        arrived(2, g + 1)
+        pieces = [1 + g * PARTS + part for part in range(PARTS)]
+        pass_on(pieces[0])
+        picked = [correlate(0, own, g)]
+        for piece in pieces[1:]:
+            pass_on(piece)
+        for piece in pieces:
+            arrived(0, piece)
+            arrived(2, piece)
         for d in range(1, ROUNDS + 1):
-            correlate(d, inbox.at[d - 1], g)
-
-    def give_back(d):
-        return pltpu.make_async_remote_copy(
-            src_ref=outgoing.at[d - 1],
-            dst_ref=returned.at[d - 1],
-            send_sem=back_send.at[d - 1],
-            recv_sem=back_recv.at[d - 1],
-            device_id={"sta": at(-d)},
-            device_id_type=pl.DeviceIdType.MESH,
-        )
-
-    for d in range(ROUNDS, 0, -1):
+            picked.append(correlate(d, inbox.at[d - 1], g))
+            outgoing[d - 1, g] = picked[d]
+            give_back(d, g).start()
+        place(0, picked, g)
+
+        @pl.when(g >= LAG)
+        def _():
+            take_back(g - LAG)
+
+    for g in range(groups - LAG, groups):
+        take_back(g)
+
+    for q in range(2 * ROUNDS + 1):
+        d = ROUNDS - q if q <= ROUNDS else q
         for part in range(2):
             for b in range(channels):
                 value = gathered[d, part * TILE : (part + 1) * TILE, b * bins : (b + 1) * bins]
-                outgoing[d - 1, part, b] = (value if part == 0 else -value).astype(jnp.bfloat16)
-        give_back(d).start()
-    for d in range(ROUNDS + 1):
-        for part in range(2):
-            for b in range(channels):
-                value = gathered[d, part * TILE : (part + 1) * TILE, b * bins : (b + 1) * bins]
-                lower[ROUNDS - d, part, b] = value.astype(jnp.bfloat16)
-
-    for piece in range(groups + 1):
+                if q > ROUNDS and part == 1:
+                    value = -value
+                result[q, part, b] = value.astype(jnp.bfloat16)
+
+    @pl.loop(0, groups)
+    def _(g):
+        for d in range(1, ROUNDS + 1):
+            give_back(d, g).wait_send()
+
+    def sent(piece):
         ahead(piece).wait_send()
         beside(piece).wait_send()
         relay_twin(piece).wait_send()
@@ -257,9 +305,11 @@
         def _():
             relay_down(piece).wait_send()
 
-    for d in range(ROUNDS, 0, -1):
-        give_back(d).wait()
-    upper[...] = returned[...]
+    sent(0)
+
+    @pl.loop(0, groups * PARTS)
+    def _(i):
+        sent(i + 1)
 
 
 def per_device(count, records, counts, gap_mask):
@@ -271,37 +321,42 @@
     blocks = 1 + groups * channels
     wide = hours * LANES
     dims = (channels, segments, samples, stations, hours, count)
-    vmem = pl.BlockSpec(memory_space=pltpu.VMEM)
-    lower, upper = pl.pallas_call(
+    pieces = groups * PARTS + 1
+    result = pl.pallas_call(
         functools.partial(kernel, dims),
-        out_shape=(
-            jax.ShapeDtypeStruct((ROUNDS + 1, 2, channels, TILE, bins), jnp.bfloat16),
-            jax.ShapeDtypeStruct((ROUNDS, 2, channels, TILE, bins), jnp.bfloat16),
-        ),
-        in_specs=[vmem] * 6,
-        out_specs=(vmem, vmem),
+        out_shape=jax.ShapeDtypeStruct((2 * ROUNDS + 1, 2, channels, TILE, bins), jnp.bfloat16),
+        in_specs=[pl.BlockSpec(memory_space=pl.ANY)] * 6,
+        out_specs=pl.BlockSpec(memory_space=pltpu.VMEM),
         scratch_shapes=[
+            pltpu.VMEM((samples, samples), jnp.bfloat16),
+            pltpu.VMEM((2 * TILE, 2 * rows), jnp.bfloat16),
+            pltpu.VMEM((rows, channels * bins), jnp.bfloat16),
+            pltpu.VMEM((channels, segments, samples), jnp.bfloat16),
+            pltpu.VMEM((stations, hours), jnp.int32),
+            pltpu.VMEM((stations, segments), jnp.int32),
             pltpu.VMEM((blocks, TILE, wide), jnp.bfloat16),
             pltpu.VMEM((blocks - 1, TILE, wide), jnp.bfloat16),
             pltpu.VMEM((ROUNDS + 1, blocks, TILE, wide), jnp.bfloat16),
             pltpu.VMEM((ROUNDS + 1, hours, rows, rows), jnp.float32),
-            pltpu.VMEM((ROUNDS + 1, 2 * TILE, channels * bins), jnp.float32),
-            pltpu.VMEM((ROUNDS, 2, channels, TILE, bins), jnp.bfloat16),
-            pltpu.VMEM((ROUNDS, 2, channels, TILE, bins), jnp.bfloat16),
-            pltpu.SemaphoreType.DMA((4, groups + 1)),
-            pltpu.SemaphoreType.DMA((4, groups + 1)),
-            pltpu.SemaphoreType.DMA((ROUNDS,)),
-            pltpu.SemaphoreType.DMA((ROUNDS,)),
+            pltpu.VMEM((2 * ROUNDS + 1, 2 * TILE, channels * bins), jnp.float32),
+            pltpu.VMEM((ROUNDS, groups, 2 * TILE, rows), jnp.bfloat16),
+            pltpu.VMEM((ROUNDS, groups, 2 * TILE, rows), jnp.bfloat16),
+            pltpu.SemaphoreType.DMA((5 + channels,)),
+            pltpu.SemaphoreType.DMA((4, pieces)),
+            pltpu.SemaphoreType.DMA((4, pieces)),
+            pltpu.SemaphoreType.DMA((ROUNDS, groups)),
+            pltpu.SemaphoreType.DMA((ROUNDS, groups)),
         ],
         compiler_params=pltpu.CompilerParams(
-            collective_id=0, has_side_effects=True, vmem_limit_bytes=48 * 1024 * 1024
+            collective_id=0, has_side_effects=True, vmem_limit_bytes=60 * 1024 * 1024
         ),
     )(
         fourier_rows(samples), pick_rows(channels), spread_bins(channels, bins),
         records, counts, gap_mask,
     )
-    below = jnp.transpose(lower[:, :, :, :channels], (0, 1, 3, 2, 4))
-    return jnp.concatenate([below, upper[:, :, :, :channels]], axis=0)
+    result = result[:, :, :, :channels]
+    below = jnp.transpose(result[: ROUNDS + 1], (0, 1, 3, 2, 4))
+    return jnp.concatenate([below, result[ROUNDS + 1 :]], axis=0)
 
 
 def solution(mesh):

time: 66.5 us -> 81.5 us (1.23)
  Pallas kernels: 59.2 us -> 77.2 us
  local copies, waits for them, and re-layouts: 6.89 us -> 3.39 us
    pallas_call x1, Pallas kernels: 59.2 us -> 77.2 us  [per_device(): pl.pallas_call(functools.partial(kernel, dims), out_shape=jax.ShapeDtypeS...]
    unnamed x12 -> x0, local copies, waits for them, and re-layouts: 5.48 us -> none
    transpose x1, local copies, waits for them, and re-layouts: 0.03 us -> 1.02 us  [per_device(): below = jnp.transpose(result[:ROUNDS + 1], (0, 1, 3, 2, 4))]
    slice x1 -> x2, local copies, waits for them, and re-layouts: 0.07 us -> 1.05 us  [per_device(): return jnp.concatenate([below, result[ROUNDS + 1:]], axis=0)]
where the time goes in v2:
time: 81.5 us; the launch traced here: 80.8 us
  Pallas kernels  77.2 us (95%)
  local copies, waits for them, and re-layouts  3.39 us (4%)
    pallas_call x1, Pallas kernels, per_device(): pl.pallas_call(functools.partial(kernel, dims), out_shape=jax.ShapeDtypeS...  77.2 us

profile of v2, /device:TPU:0, one launch (start us, length us, event | category | flops | bytes accessed | tf_op | source)
XLA Modules:
  0.0 80.8 jit_solution(5824383990077692541)
XLA Ops:
  0.0 77.2 %shard_map.64 = bf16[7,2,12,16,128]{4,3,2,1,0:T(8,128)(2,1)} custom-call(bf16[256,256]{1,0:T(8,128)(2,1)} %constant.6.clone.table_in, bf16[32,384]{1,0:T(8,128)(2,1)} %constant.7.clone.pick_in, bf16[192,1536]{1,0:T(8,128)(2,1)} %constant.8.clone.spread_in, bf16[12,256,256]{2,1,0:T(8,128)(2,1)} %records_in.1, s32[4,4]{1,0:T(4,128)} %counts_in.1, s32[4,256]{1,0:T(4,128)} %gaps_in.1), custom_call_target="tpu_custom_call" | custom-call | tf_op jit(solution)/shard_map/pallas_call | solution.py:325
  77.2 1.0 %slice.10 = bf16[3,2,12,12,128]{4,3,2,1,0:T(8,128)(2,1)S(1)} slice(bf16[7,2,12,16,128]{4,3,2,1,0:T(8,128)(2,1)} %shard_map.64), slice={[4:7], [0:2], [0:12], [0:12], [0:128]} | slice | bytes 442368 | tf_op jit(solution)/shard_map/slice | solution.py:359
  78.2 1.0 %slice_bitcast_fusion = bf16[4,2,12,12,128]{4,2,3,1,0:T(8,128)(2,1)S(1)} fusion(bf16[7,2,12,16,128]{4,3,2,1,0:T(8,128)(2,1)} %shard_map.64), kind=kLoop, calls=%fused_computation.1 | loop fusion | bytes 589824 | tf_op jit(solution)/shard_map/transpose | solution.py:358
  79.2 0.1 copy.7
  79.3 0.1 pad_maximum_fusion
  79.4 1.3 %copy.8 = bf16[7,2,12,12,128]{4,1,3,2,0:T(2,128)(2,1)} copy(bf16[7,2,12,12,128]{4,2,3,1,0:T(8,128)(2,1)S(1)} %pad_maximum_fusion) | data formatting | bytes 1032192 | tf_op jit(solution)/shard_map/concatenate | solution.py:359

commit v3 on v2

--- a/solution.py
+++ b/solution.py
@@ -13,6 +13,7 @@
 LANES = 128
 PARTS = 2
 LAG = 2
+COLS = 256
 EPSILON = 1e-06
 NT = (((1,), (1,)), ((), ()))
 
@@ -47,7 +48,7 @@
 def kernel(
     dims, table_in, pick_in, spread_in, records_in, counts_in, gaps_in, result,
     table, pick, spread, records, counts, gaps,
-    own, turned, inbox, weights, gathered, outgoing, returned,
+    own, turned, inbox, weights, gathered, selves, outgoing, returned,
     load_sem, send_sem, recv_sem, back_send, back_recv,
 ):
     channels, segments, samples, stations, hours, count = dims
@@ -196,9 +197,18 @@
     def dot_nt(a, b):
         return lax.dot_general(a, b, NT, preferred_element_type=jnp.float32)
 
-    row_id = lax.broadcasted_iota(jnp.int32, (rows, rows), 0)
-    col_id = lax.broadcasted_iota(jnp.int32, (rows, rows), 1)
-    diagonal = lax.rem(row_id, TILE) == lax.rem(col_id, TILE)
+    partners = (own,) + tuple(inbox.at[d] for d in range(ROUNDS))
+    chunks = (ROUNDS + 1) * rows // COLS
+    each = COLS // TILE
+
+    def columns(blocks, n):
+        out = []
+        for d, block in enumerate(blocks):
+            first = max(each * n, d * channels) - d * channels
+            last = min(each * (n + 1), (d + 1) * channels) - d * channels
+            if first < last:
+                out.append(block[first * TILE : last * TILE])
+        return jnp.concatenate(out, axis=0) if len(out) > 1 else out[0]
 
     def widen(ref, h):
         block = ref[0, :, h * LANES : (h + 1) * LANES].astype(jnp.float32)
@@ -206,28 +216,36 @@
             [jnp.broadcast_to(block[c : c + 1], (TILE, LANES)) for c in range(channels)], axis=0
         ).astype(jnp.bfloat16)
 
-    def weigh(d, partner):
+    def weigh():
+        row_id = lax.broadcasted_iota(jnp.int32, (rows, COLS), 0)
+        col_id = lax.broadcasted_iota(jnp.int32, (rows, COLS), 1)
+        diagonal = lax.rem(row_id, TILE) == lax.rem(col_id, TILE)
         for h in range(hours):
-            joint = dot_nt(widen(own, h), widen(partner, h))
-            weights[d, h] = jnp.where(diagonal, 1.0 / (hours * jnp.maximum(joint, 1.0)), 0.0)
+            wide = [widen(ref, h) for ref in partners]
+            for n in range(chunks):
+                joint = dot_nt(wide[0], columns(wide, n))
+                weights[h, n] = jnp.where(diagonal, 1.0 / (hours * jnp.maximum(joint, 1.0)), 0.0)
 
     lane_group = lax.rem(lax.broadcasted_iota(jnp.int32, (2 * TILE, channels * bins), 1), bins) // TILE
 
-    def correlate(d, partner, g):
+    def correlate(g):
         at_rows = pl.ds(1 + g * channels, channels)
         t_rows = pl.ds(g * channels, channels)
-        re = jnp.zeros((rows, rows), jnp.float32)
-        im = jnp.zeros((rows, rows), jnp.float32)
-        for h in range(hours):
-            lanes = slice(h * LANES, (h + 1) * LANES)
-            other = partner[at_rows, :, lanes].reshape(rows, LANES)
-            mine = own[at_rows, :, lanes].reshape(rows, LANES)
-            mine_t = turned[t_rows, :, lanes].reshape(rows, LANES)
-            scale = weights[d, h]
-            re = re + dot_nt(mine, other) * scale
-            im = im + dot_nt(mine_t, other) * scale
-        both = jnp.concatenate([re, im], axis=0).astype(jnp.bfloat16)
-        return jnp.dot(pick[...], both, preferred_element_type=jnp.float32).astype(jnp.bfloat16)
+        picked = []
+        for n in range(chunks):
+            re = jnp.zeros((rows, COLS), jnp.float32)
+            im = jnp.zeros((rows, COLS), jnp.float32)
+            for h in range(hours):
+                lanes = slice(h * LANES, (h + 1) * LANES)
+                blocks = [ref[at_rows, :, lanes].reshape(rows, LANES) for ref in partners]
+                mine_t = turned[t_rows, :, lanes].reshape(rows, LANES)
+                product = dot_nt(jnp.concatenate([blocks[0], mine_t], axis=0), columns(blocks, n))
+                scale = weights[h, n]
+                re = re + product[:rows] * scale
+                im = im + product[rows:] * scale
+            both = jnp.concatenate([re, im], axis=0).astype(jnp.bfloat16)
+            picked.append(jnp.dot(pick[...], both, preferred_element_type=jnp.float32))
+        return jnp.concatenate(picked, axis=1)
 
     def give_back(d, g):
         return pltpu.make_async_remote_copy(
@@ -239,48 +257,44 @@
             device_id_type=pl.DeviceIdType.MESH,
         )
 
-    def place(first, picked, g):
-        wide = jnp.dot(
-            jnp.concatenate(picked, axis=0), spread[...], preferred_element_type=jnp.float32
-        )
-        for i in range(len(picked)):
-            rows_i = wide[i * 2 * TILE : (i + 1) * 2 * TILE]
-            gathered[first + i] = jnp.where(lane_group == g, rows_i, gathered[first + i])
-
-    def take_back(g):
+    def place(g):
         for d in range(1, ROUNDS + 1):
             give_back(d, g).wait_recv()
-        place(ROUNDS + 1, [returned[d - 1, g] for d in range(1, ROUNDS + 1)], g)
-
-    weigh(0, own)
+        parts = [selves[g]]
+        parts += [outgoing[d, g] for d in range(ROUNDS)]
+        parts += [returned[d, g] for d in range(ROUNDS)]
+        wide = jnp.dot(
+            jnp.concatenate(parts, axis=0), spread[...], preferred_element_type=jnp.float32
+        )
+        for i in range(len(parts)):
+            rows_i = wide[i * 2 * TILE : (i + 1) * 2 * TILE]
+            gathered[i] = jnp.where(lane_group == g, rows_i, gathered[i])
+
     pass_on(0)
     arrived(0, 0)
     arrived(2, 0)
-    for d in range(1, ROUNDS + 1):
-        weigh(d, inbox.at[d - 1])
+    weigh()
 
     @pl.loop(0, groups)
     def _(g):
         pieces = [1 + g * PARTS + part for part in range(PARTS)]
-        pass_on(pieces[0])
-        picked = [correlate(0, own, g)]
-        for piece in pieces[1:]:
+        for piece in pieces:
             pass_on(piece)
         for piece in pieces:
             arrived(0, piece)
             arrived(2, piece)
+        picked = correlate(g)
         for d in range(1, ROUNDS + 1):
-            picked.append(correlate(d, inbox.at[d - 1], g))
-            outgoing[d - 1, g] = picked[d]
+            outgoing[d - 1, g] = picked[:, d * rows : (d + 1) * rows].astype(jnp.bfloat16)
             give_back(d, g).start()
-        place(0, picked, g)
+        selves[g] = picked[:, :rows].astype(jnp.bfloat16)
 
         @pl.when(g >= LAG)
         def _():
-            take_back(g - LAG)
+            place(g - LAG)
 
     for g in range(groups - LAG, groups):
-        take_back(g)
+        place(g)
 
     for q in range(2 * ROUNDS + 1):
         d = ROUNDS - q if q <= ROUNDS else q
@@ -325,7 +339,7 @@
     result = pl.pallas_call(
         functools.partial(kernel, dims),
         out_shape=jax.ShapeDtypeStruct((2 * ROUNDS + 1, 2, channels, TILE, bins), jnp.bfloat16),
-        in_specs=[pl.BlockSpec(memory_space=pl.ANY)] * 6,
+        in_specs=[pl.BlockSpec(memory_space=pltpu.HBM)] * 6,
         out_specs=pl.BlockSpec(memory_space=pltpu.VMEM),
         scratch_shapes=[
             pltpu.VMEM((samples, samples), jnp.bfloat16),
@@ -337,8 +351,9 @@
             pltpu.VMEM((blocks, TILE, wide), jnp.bfloat16),
             pltpu.VMEM((blocks - 1, TILE, wide), jnp.bfloat16),
             pltpu.VMEM((ROUNDS + 1, blocks, TILE, wide), jnp.bfloat16),
-            pltpu.VMEM((ROUNDS + 1, hours, rows, rows), jnp.float32),
+            pltpu.VMEM((hours, (ROUNDS + 1) * rows // COLS, rows, COLS), jnp.float32),
             pltpu.VMEM((2 * ROUNDS + 1, 2 * TILE, channels * bins), jnp.float32),
+            pltpu.VMEM((groups, 2 * TILE, rows), jnp.bfloat16),
             pltpu.VMEM((ROUNDS, groups, 2 * TILE, rows), jnp.bfloat16),
             pltpu.VMEM((ROUNDS, groups, 2 * TILE, rows), jnp.bfloat16),
             pltpu.SemaphoreType.DMA((5 + channels,)),
@@ -348,7 +363,7 @@
             pltpu.SemaphoreType.DMA((ROUNDS, groups)),
         ],
         compiler_params=pltpu.CompilerParams(
-            collective_id=0, has_side_effects=True, vmem_limit_bytes=60 * 1024 * 1024
+            collective_id=0, has_side_effects=True, vmem_limit_bytes=54 * 1024 * 1024
         ),
     )(
         fourier_rows(samples), pick_rows(channels), spread_bins(channels, bins),

time: 81.5 us -> 80.9 us (level)
  no operation moved by 1% of the time
where the time goes in v3:
time: 80.9 us; the launch traced here: 80.7 us
  Pallas kernels  77.1 us (95%)
  local copies, waits for them, and re-layouts  3.39 us (4%)
    pallas_call x1, Pallas kernels, per_device(): pl.pallas_call(functools.partial(kernel, dims), out_shape=jax.ShapeDtypeS...  77.1 us

profile of v3, /device:TPU:0, one launch (start us, length us, event | category | flops | bytes accessed | tf_op | source)
XLA Modules:
  0.0 80.7 jit_solution(10667279993824002003)
XLA Ops:
  0.0 77.1 %shard_map.64 = bf16[7,2,12,16,128]{4,3,2,1,0:T(8,128)(2,1)} custom-call(bf16[256,256]{1,0:T(8,128)(2,1)} %constant.6.clone.table_in, bf16[32,384]{1,0:T(8,128)(2,1)} %constant.7.clone.pick_in, bf16[192,1536]{1,0:T(8,128)(2,1)} %constant.8.clone.spread_in, bf16[12,256,256]{2,1,0:T(8,128)(2,1)} %records_in.1, s32[4,4]{1,0:T(4,128)} %counts_in.1, s32[4,256]{1,0:T(4,128)} %gaps_in.1), custom_call_target="tpu_custom_call" | custom-call | tf_op jit(solution)/shard_map/pallas_call | solution.py:339
  77.1 1.0 %slice.10 = bf16[3,2,12,12,128]{4,3,2,1,0:T(8,128)(2,1)S(1)} slice(bf16[7,2,12,16,128]{4,3,2,1,0:T(8,128)(2,1)} %shard_map.64), slice={[4:7], [0:2], [0:12], [0:12], [0:128]} | slice | bytes 442368 | tf_op jit(solution)/shard_map/slice | solution.py:374
  78.1 1.0 %slice_bitcast_fusion = bf16[4,2,12,12,128]{4,2,3,1,0:T(8,128)(2,1)S(1)} fusion(bf16[7,2,12,16,128]{4,3,2,1,0:T(8,128)(2,1)} %shard_map.64), kind=kLoop, calls=%fused_computation.1 | loop fusion | bytes 589824 | tf_op jit(solution)/shard_map/transpose | solution.py:373
  79.1 0.1 copy.7
  79.2 0.1 pad_maximum_fusion
  79.3 1.3 %copy.8 = bf16[7,2,12,12,128]{4,1,3,2,0:T(2,128)(2,1)} copy(bf16[7,2,12,12,128]{4,2,3,1,0:T(8,128)(2,1)S(1)} %pad_maximum_fusion) | data formatting | bytes 1032192 | tf_op jit(solution)/shard_map/concatenate | solution.py:374

commit v4 on v3

--- a/solution.py
+++ b/solution.py
@@ -11,8 +11,7 @@
 ROUNDS = 3
 TILE = 16
 LANES = 128
-PARTS = 2
-LAG = 2
+PARTS = 1
 COLS = 256
 EPSILON = 1e-06
 NT = (((1,), (1,)), ((), ()))
@@ -48,7 +47,7 @@
 def kernel(
     dims, table_in, pick_in, spread_in, records_in, counts_in, gaps_in, result,
     table, pick, spread, records, counts, gaps,
-    own, turned, inbox, weights, gathered, selves, outgoing, returned,
+    own, turned, inbox, weights, outgoing, returned,
     load_sem, send_sem, recv_sem, back_send, back_recv,
 ):
     channels, segments, samples, stations, hours, count = dims
@@ -90,7 +89,6 @@
     for load in record_loads:
         load.start()
     barrier_signal()
-    gathered[...] = jnp.zeros_like(gathered)
     for load in loads:
         load.wait()
 
@@ -226,8 +224,6 @@
                 joint = dot_nt(wide[0], columns(wide, n))
                 weights[h, n] = jnp.where(diagonal, 1.0 / (hours * jnp.maximum(joint, 1.0)), 0.0)
 
-    lane_group = lax.rem(lax.broadcasted_iota(jnp.int32, (2 * TILE, channels * bins), 1), bins) // TILE
-
     def correlate(g):
         at_rows = pl.ds(1 + g * channels, channels)
         t_rows = pl.ds(g * channels, channels)
@@ -247,28 +243,37 @@
             picked.append(jnp.dot(pick[...], both, preferred_element_type=jnp.float32))
         return jnp.concatenate(picked, axis=1)
 
+    tall = 2 * TILE
+
     def give_back(d, g):
         return pltpu.make_async_remote_copy(
-            src_ref=outgoing.at[d - 1, g],
-            dst_ref=returned.at[d - 1, g],
+            src_ref=outgoing.at[g, pl.ds(d * tall, tall)],
+            dst_ref=returned.at[g, pl.ds((d - 1) * tall, tall)],
             send_sem=back_send.at[d - 1, g],
             recv_sem=back_recv.at[d - 1, g],
             device_id={"sta": at(-d)},
             device_id_type=pl.DeviceIdType.MESH,
         )
 
-    def place(g):
-        for d in range(1, ROUNDS + 1):
-            give_back(d, g).wait_recv()
-        parts = [selves[g]]
-        parts += [outgoing[d, g] for d in range(ROUNDS)]
-        parts += [returned[d, g] for d in range(ROUNDS)]
-        wide = jnp.dot(
-            jnp.concatenate(parts, axis=0), spread[...], preferred_element_type=jnp.float32
-        )
-        for i in range(len(parts)):
-            rows_i = wide[i * 2 * TILE : (i + 1) * 2 * TILE]
-            gathered[i] = jnp.where(lane_group == g, rows_i, gathered[i])
+    def finish(ref, slots):
+        height = len(slots) * tall
+        group_of = lax.rem(lax.broadcasted_iota(jnp.int32, (height, COLS), 1), bins) // TILE
+        flat = ref[...].reshape(groups * height, rows)
+        for n in range(channels * bins // COLS):
+            wide = jnp.dot(
+                flat, spread[:, n * COLS : (n + 1) * COLS], preferred_element_type=jnp.float32
+            )
+            merged = wide[:height]
+            for g in range(1, groups):
+                merged = jnp.where(group_of == g, wide[g * height : (g + 1) * height], merged)
+            for i, (slot, flip) in enumerate(slots):
+                for part in range(2):
+                    for k in range(COLS // bins):
+                        start = i * tall + part * TILE
+                        value = merged[start : start + TILE, k * bins : (k + 1) * bins]
+                        if flip and part == 1:
+                            value = -value
+                        result[slot, part, n * (COLS // bins) + k] = value.astype(jnp.bfloat16)
 
     pass_on(0)
     arrived(0, 0)
@@ -285,25 +290,20 @@
             arrived(2, piece)
         picked = correlate(g)
         for d in range(1, ROUNDS + 1):
-            outgoing[d - 1, g] = picked[:, d * rows : (d + 1) * rows].astype(jnp.bfloat16)
+            outgoing[g, d * tall : (d + 1) * tall] = picked[:, d * rows : (d + 1) * rows].astype(
+                jnp.bfloat16
+            )
             give_back(d, g).start()
-        selves[g] = picked[:, :rows].astype(jnp.bfloat16)
-
-        @pl.when(g >= LAG)
-        def _():
-            place(g - LAG)
-
-    for g in range(groups - LAG, groups):
-        place(g)
-
-    for q in range(2 * ROUNDS + 1):
-        d = ROUNDS - q if q <= ROUNDS else q
-        for part in range(2):
-            for b in range(channels):
-                value = gathered[d, part * TILE : (part + 1) * TILE, b * bins : (b + 1) * bins]
-                if q > ROUNDS and part == 1:
-                    value = -value
-                result[q, part, b] = value.astype(jnp.bfloat16)
+        outgoing[g, :tall] = picked[:, :rows].astype(jnp.bfloat16)
+
+    finish(outgoing, [(ROUNDS - d, False) for d in range(ROUNDS + 1)])
+
+    @pl.loop(0, groups)
+    def _(g):
+        for d in range(1, ROUNDS + 1):
+            give_back(d, g).wait_recv()
+
+    finish(returned, [(ROUNDS + d, True) for d in range(1, ROUNDS + 1)])
 
     @pl.loop(0, groups)
     def _(g):
@@ -352,10 +352,8 @@
             pltpu.VMEM((blocks - 1, TILE, wide), jnp.bfloat16),
             pltpu.VMEM((ROUNDS + 1, blocks, TILE, wide), jnp.bfloat16),
             pltpu.VMEM((hours, (ROUNDS + 1) * rows // COLS, rows, COLS), jnp.float32),
-            pltpu.VMEM((2 * ROUNDS + 1, 2 * TILE, channels * bins), jnp.float32),
-            pltpu.VMEM((groups, 2 * TILE, rows), jnp.bfloat16),
-            pltpu.VMEM((ROUNDS, groups, 2 * TILE, rows), jnp.bfloat16),
-            pltpu.VMEM((ROUNDS, groups, 2 * TILE, rows), jnp.bfloat16),
+            pltpu.VMEM((groups, (ROUNDS + 1) * 2 * TILE, rows), jnp.bfloat16),
+            pltpu.VMEM((groups, ROUNDS * 2 * TILE, rows), jnp.bfloat16),
             pltpu.SemaphoreType.DMA((5 + channels,)),
             pltpu.SemaphoreType.DMA((4, pieces)),
             pltpu.SemaphoreType.DMA((4, pieces)),

time: 80.9 us -> 67.2 us (0.83)
  Pallas kernels: 77.1 us -> 63.3 us
    pallas_call x1, Pallas kernels: 77.1 us -> 63.3 us  [per_device(): pl.pallas_call(functools.partial(kernel, dims), out_shape=jax.ShapeDtypeS...]
where the time goes in v4:
time: 67.2 us; the launch traced here: 66.8 us
  Pallas kernels  63.3 us (94%)
  local copies, waits for them, and re-layouts  3.39 us (5%)
    pallas_call x1, Pallas kernels, per_device(): pl.pallas_call(functools.partial(kernel, dims), out_shape=jax.ShapeDtypeS...  63.3 us

profile of v4, /device:TPU:0, one launch (start us, length us, event | category | flops | bytes accessed | tf_op | source)
XLA Modules:
  0.0 66.8 jit_solution(8643234339745954484)
XLA Ops:
  0.0 63.3 %shard_map.64 = bf16[7,2,12,16,128]{4,3,2,1,0:T(8,128)(2,1)} custom-call(bf16[256,256]{1,0:T(8,128)(2,1)} %constant.6.clone.table_in, bf16[32,384]{1,0:T(8,128)(2,1)} %constant.7.clone.pick_in, bf16[192,1536]{1,0:T(8,128)(2,1)} %constant.8.clone.spread_in, bf16[12,256,256]{2,1,0:T(8,128)(2,1)} %records_in.1, s32[4,4]{1,0:T(4,128)} %counts_in.1, s32[4,256]{1,0:T(4,128)} %gaps_in.1), custom_call_target="tpu_custom_call" | custom-call | tf_op jit(solution)/shard_map/pallas_call | solution.py:339
  63.3 1.0 %slice.10 = bf16[3,2,12,12,128]{4,3,2,1,0:T(8,128)(2,1)S(1)} slice(bf16[7,2,12,16,128]{4,3,2,1,0:T(8,128)(2,1)} %shard_map.64), slice={[4:7], [0:2], [0:12], [0:12], [0:128]} | slice | bytes 442368 | tf_op jit(solution)/shard_map/slice | solution.py:372
  64.3 1.0 %slice_bitcast_fusion = bf16[4,2,12,12,128]{4,2,3,1,0:T(8,128)(2,1)S(1)} fusion(bf16[7,2,12,16,128]{4,3,2,1,0:T(8,128)(2,1)} %shard_map.64), kind=kLoop, calls=%fused_computation.1 | loop fusion | bytes 589824 | tf_op jit(solution)/shard_map/transpose | solution.py:371
  65.3 0.1 copy.7
  65.4 0.1 pad_maximum_fusion
  65.5 1.3 %copy.8 = bf16[7,2,12,12,128]{4,1,3,2,0:T(2,128)(2,1)} copy(bf16[7,2,12,12,128]{4,2,3,1,0:T(8,128)(2,1)S(1)} %pad_maximum_fusion) | data formatting | bytes 1032192 | tf_op jit(solution)/shard_map/concatenate | solution.py:372

commit v5 on v4

--- a/solution.py
+++ b/solution.py
@@ -11,7 +11,7 @@
 ROUNDS = 3
 TILE = 16
 LANES = 128
-PARTS = 1
+PARTS = 2
 COLS = 256
 EPSILON = 1e-06
 NT = (((1,), (1,)), ((), ()))
@@ -59,7 +59,7 @@
     me = lax.axis_index("sta")
     kind = lax.rem(me, 4)
     core = lax.rem(kind, 2)
-    side = kind // 2
+    far = kind // 3
 
     def at(offset):
         return lax.rem(me + offset + count, count)
@@ -151,7 +151,7 @@
         )
 
     def ahead(piece):
-        return copy(own, piece, 0, 1 + 2 * side, at(2 + 2 * side))
+        return copy(own, piece, 0, 1 + 2 * far, at(2 + 2 * far))
 
     def beside(piece):
         return copy(own, piece, 1, 2 * core, at(1 + 2 * core))
@@ -171,18 +171,15 @@
     def send_own(piece):
         ahead(piece).start()
 
-        @pl.when(kind != 3)
+        @pl.when(far == 0)
         def _():
             beside(piece).start()
 
     def pass_on(piece):
-        @pl.when(side == 1)
+        @pl.when(far == 1)
         def _():
             arrived(3, piece)
             relay_down(piece).start()
-
-        @pl.when(kind == 3)
-        def _():
             relay_twin_far(piece).start()
 
         arrived(1, piece)
@@ -315,7 +312,7 @@
         beside(piece).wait_send()
         relay_twin(piece).wait_send()
 
-        @pl.when(side == 1)
+        @pl.when(far == 1)
         def _():
             relay_down(piece).wait_send()
 

time: 67.2 us -> 64.1 us (0.954)
  Pallas kernels: 63.3 us -> 60.3 us
    pallas_call x1, Pallas kernels: 63.3 us -> 60.3 us  [per_device(): pl.pallas_call(functools.partial(kernel, dims), out_shape=jax.ShapeDtypeS...]
where the time goes in v5:
time: 64.1 us; the launch traced here: 63.9 us
  Pallas kernels  60.3 us (94%)
  local copies, waits for them, and re-layouts  3.39 us (5%)
    pallas_call x1, Pallas kernels, per_device(): pl.pallas_call(functools.partial(kernel, dims), out_shape=jax.ShapeDtypeS...  60.3 us
    concatenate x1, local copies, waits for them, and re-layouts, per_device(): return jnp.concatenate([below, result[ROUNDS + 1:]], axis=0)  1.32 us

profile of v5, /device:TPU:0, one launch (start us, length us, event | category | flops | bytes accessed | tf_op | source)
XLA Modules:
  0.0 63.9 jit_solution(8333778709551184660)
XLA Ops:
  0.0 60.3 %shard_map.64 = bf16[7,2,12,16,128]{4,3,2,1,0:T(8,128)(2,1)} custom-call(bf16[256,256]{1,0:T(8,128)(2,1)} %constant.6.clone.table_in, bf16[32,384]{1,0:T(8,128)(2,1)} %constant.7.clone.pick_in, bf16[192,1536]{1,0:T(8,128)(2,1)} %constant.8.clone.spread_in, bf16[12,256,256]{2,1,0:T(8,128)(2,1)} %records_in.1, s32[4,4]{1,0:T(4,128)} %counts_in.1, s32[4,256]{1,0:T(4,128)} %gaps_in.1), custom_call_target="tpu_custom_call" | custom-call | tf_op jit(solution)/shard_map/pallas_call | solution.py:336
  60.3 1.0 %slice.10 = bf16[3,2,12,12,128]{4,3,2,1,0:T(8,128)(2,1)S(1)} slice(bf16[7,2,12,16,128]{4,3,2,1,0:T(8,128)(2,1)} %shard_map.64), slice={[4:7], [0:2], [0:12], [0:12], [0:128]} | slice | bytes 442368 | tf_op jit(solution)/shard_map/slice | solution.py:369
  61.3 1.0 %slice_bitcast_fusion = bf16[4,2,12,12,128]{4,2,3,1,0:T(8,128)(2,1)S(1)} fusion(bf16[7,2,12,16,128]{4,3,2,1,0:T(8,128)(2,1)} %shard_map.64), kind=kLoop, calls=%fused_computation.1 | loop fusion | bytes 589824 | tf_op jit(solution)/shard_map/transpose | solution.py:368
  62.3 0.1 copy.7
  62.4 0.1 pad_maximum_fusion
  62.5 1.3 %copy.8 = bf16[7,2,12,12,128]{4,1,3,2,0:T(2,128)(2,1)} copy(bf16[7,2,12,12,128]{4,2,3,1,0:T(8,128)(2,1)S(1)} %pad_maximum_fusion) | data formatting | bytes 1032192 | tf_op jit(solution)/shard_map/concatenate | solution.py:369

commit v6 on v5

--- a/solution.py
+++ b/solution.py
@@ -13,6 +13,8 @@
 LANES = 128
 PARTS = 2
 COLS = 256
+EARLY = 2
+TURN = 4
 EPSILON = 1e-06
 NT = (((1,), (1,)), ((), ()))
 
@@ -89,6 +91,7 @@
     for load in record_loads:
         load.start()
     barrier_signal()
+    part_rows = channels // PARTS
     for load in loads:
         load.wait()
 
@@ -110,31 +113,6 @@
         own[0, :, 2 * pair * LANES : (2 * pair + 1) * LANES] = first.astype(jnp.bfloat16)
         own[0, :, (2 * pair + 1) * LANES : (2 * pair + 2) * LANES] = second.astype(jnp.bfloat16)
 
-    left_b = lax.broadcasted_iota(jnp.int32, (bins, LANES), 1) < span
-    for c in range(channels):
-        record_loads[c].wait()
-        spectrum = lax.dot_general(table[...], records[c], NT, preferred_element_type=jnp.float32)
-        power = jnp.sum(spectrum * spectrum, axis=0, keepdims=True) * (1.0 / samples)
-        white = spectrum * (lax.rsqrt(power + EPSILON) * valid[c : c + 1])
-        for pair in range(hours // 2):
-            re = white[:bins, pair * LANES : (pair + 1) * LANES]
-            im = white[bins:, pair * LANES : (pair + 1) * LANES]
-            re_r = pltpu.roll(re, span, 1)
-            im_r = pltpu.roll(im, span, 1)
-            straight = (jnp.where(left_b, re, im_r), jnp.where(left_b, re_r, im))
-            across = (jnp.where(left_b, im, -re_r), jnp.where(left_b, im_r, -re))
-            for half in range(2):
-                lanes = slice((2 * pair + half) * LANES, (2 * pair + half + 1) * LANES)
-                flat = straight[half].astype(jnp.bfloat16)
-                flat_t = across[half].astype(jnp.bfloat16)
-                for g in range(groups):
-                    own[1 + g * channels + c, :, lanes] = flat[g * TILE : (g + 1) * TILE]
-                    turned[g * channels + c, :, lanes] = flat_t[g * TILE : (g + 1) * TILE]
-
-    pl.semaphore_wait(pltpu.get_barrier_semaphore(), 8)
-
-    part_rows = channels // PARTS
-
     def where_is(piece):
         if isinstance(piece, int) and piece == 0:
             return pl.ds(0, 1)
@@ -185,9 +163,47 @@
         arrived(1, piece)
         relay_twin(piece).start()
 
-    send_own(0)
-    for piece in range(groups * PARTS):
+    left_b = lax.broadcasted_iota(jnp.int32, (bins, LANES), 1) < span
+
+    def whiten(c):
+        record_loads[c].wait()
+        spectrum = lax.dot_general(table[...], records[c], NT, preferred_element_type=jnp.float32)
+        power = jnp.sum(spectrum * spectrum, axis=0, keepdims=True) * (1.0 / samples)
+        white = spectrum * (lax.rsqrt(power + EPSILON) * valid[c : c + 1])
+        for pair in range(hours // 2):
+            re = white[:bins, pair * LANES : (pair + 1) * LANES]
+            im = white[bins:, pair * LANES : (pair + 1) * LANES]
+            straight = (
+                jnp.where(left_b, re, pltpu.roll(im, span, 1)),
+                jnp.where(left_b, pltpu.roll(re, span, 1), im),
+            )
+            for half in range(2):
+                lanes = slice((2 * pair + half) * LANES, (2 * pair + half + 1) * LANES)
+                flat = straight[half].astype(jnp.bfloat16)
+                for g in range(groups):
+                    own[1 + g * channels + c, :, lanes] = flat[g * TILE : (g + 1) * TILE]
+
+    early = min(EARLY, groups)
+    for part in range(PARTS):
+        for c in range(part * part_rows, (part + 1) * part_rows):
+            whiten(c)
+        if part == 0:
+            pl.semaphore_wait(pltpu.get_barrier_semaphore(), 8)
+            send_own(0)
+        for g in range(early):
+            send_own(1 + g * PARTS + part)
+    for piece in range(early * PARTS, groups * PARTS):
         send_own(1 + piece)
+
+    sign = jnp.where(left, 1.0, -1.0)
+
+    @pl.loop(0, groups * channels // TURN)
+    def _(i):
+        for r in range(TURN):
+            for h in range(hours):
+                lanes = slice(h * LANES, (h + 1) * LANES)
+                block = own[1 + i * TURN + r, :, lanes].astype(jnp.float32)
+                turned[i * TURN + r, :, lanes] = (pltpu.roll(block, span, 1) * sign).astype(jnp.bfloat16)
 
     def dot_nt(a, b):
         return lax.dot_general(a, b, NT, preferred_element_type=jnp.float32)

time: 64.1 us -> 62.8 us (0.980)
  Pallas kernels: 60.3 us -> 59 us
    pallas_call x1, Pallas kernels: 60.3 us -> 59 us  [per_device(): pl.pallas_call(functools.partial(kernel, dims), out_shape=jax.ShapeDtypeS...]
where the time goes in v6:
time: 62.8 us; the launch traced here: 62.6 us
  Pallas kernels  59 us (94%)
  local copies, waits for them, and re-layouts  3.39 us (5%)
    pallas_call x1, Pallas kernels, per_device(): pl.pallas_call(functools.partial(kernel, dims), out_shape=jax.ShapeDtypeS...  59 us
    concatenate x1, local copies, waits for them, and re-layouts, per_device(): return jnp.concatenate([below, result[ROUNDS + 1:]], axis=0)  1.32 us

profile of v6, /device:TPU:0, one launch (start us, length us, event | category | flops | bytes accessed | tf_op | source)
XLA Modules:
  0.0 62.6 jit_solution(6786451854696071449)
XLA Ops:
  0.0 59.0 %shard_map.64 = bf16[7,2,12,16,128]{4,3,2,1,0:T(8,128)(2,1)} custom-call(bf16[256,256]{1,0:T(8,128)(2,1)} %constant.6.clone.table_in, bf16[32,384]{1,0:T(8,128)(2,1)} %constant.7.clone.pick_in, bf16[192,1536]{1,0:T(8,128)(2,1)} %constant.8.clone.spread_in, bf16[12,256,256]{2,1,0:T(8,128)(2,1)} %records_in.1, s32[4,4]{1,0:T(4,128)} %counts_in.1, s32[4,256]{1,0:T(4,128)} %gaps_in.1), custom_call_target="tpu_custom_call" | custom-call | tf_op jit(solution)/shard_map/pallas_call | solution.py:352
  59.0 1.0 %slice.10 = bf16[3,2,12,12,128]{4,3,2,1,0:T(8,128)(2,1)S(1)} slice(bf16[7,2,12,16,128]{4,3,2,1,0:T(8,128)(2,1)} %shard_map.64), slice={[4:7], [0:2], [0:12], [0:12], [0:128]} | slice | bytes 442368 | tf_op jit(solution)/shard_map/slice | solution.py:385
  60.0 1.0 %slice_bitcast_fusion = bf16[4,2,12,12,128]{4,2,3,1,0:T(8,128)(2,1)S(1)} fusion(bf16[7,2,12,16,128]{4,3,2,1,0:T(8,128)(2,1)} %shard_map.64), kind=kLoop, calls=%fused_computation.1 | loop fusion | bytes 589824 | tf_op jit(solution)/shard_map/transpose | solution.py:384
  61.0 0.1 copy.7
  61.1 0.1 pad_maximum_fusion
  61.2 1.3 %copy.8 = bf16[7,2,12,12,128]{4,1,3,2,0:T(2,128)(2,1)} copy(bf16[7,2,12,12,128]{4,2,3,1,0:T(8,128)(2,1)S(1)} %pad_maximum_fusion) | data formatting | bytes 1032192 | tf_op jit(solution)/shard_map/concatenate | solution.py:385

commit v7 on v6

--- a/solution.py
+++ b/solution.py
@@ -11,7 +11,7 @@
 ROUNDS = 3
 TILE = 16
 LANES = 128
-PARTS = 2
+PARTS = 3
 COLS = 256
 EARLY = 2
 TURN = 4

time: 62.8 us -> 63.3 us (level)
  no operation moved by 1% of the time
where the time goes in v7:
time: 63.3 us; the launch traced here: 63 us
  Pallas kernels  59.5 us (94%)
  local copies, waits for them, and re-layouts  3.39 us (5%)
    pallas_call x1, Pallas kernels, per_device(): pl.pallas_call(functools.partial(kernel, dims), out_shape=jax.ShapeDtypeS...  59.5 us
    concatenate x1, local copies, waits for them, and re-layouts, per_device(): return jnp.concatenate([below, result[ROUNDS + 1:]], axis=0)  1.32 us

profile of v7, /device:TPU:0, one launch (start us, length us, event | category | flops | bytes accessed | tf_op | source)
XLA Modules:
  0.0 63.0 jit_solution(15838788162067743251)
XLA Ops:
  0.0 59.5 %shard_map.64 = bf16[7,2,12,16,128]{4,3,2,1,0:T(8,128)(2,1)} custom-call(bf16[256,256]{1,0:T(8,128)(2,1)} %constant.6.clone.table_in, bf16[32,384]{1,0:T(8,128)(2,1)} %constant.7.clone.pick_in, bf16[192,1536]{1,0:T(8,128)(2,1)} %constant.8.clone.spread_in, bf16[12,256,256]{2,1,0:T(8,128)(2,1)} %records_in.1, s32[4,4]{1,0:T(4,128)} %counts_in.1, s32[4,256]{1,0:T(4,128)} %gaps_in.1), custom_call_target="tpu_custom_call" | custom-call | tf_op jit(solution)/shard_map/pallas_call | solution.py:352
  59.5 1.0 %slice.10 = bf16[3,2,12,12,128]{4,3,2,1,0:T(8,128)(2,1)S(1)} slice(bf16[7,2,12,16,128]{4,3,2,1,0:T(8,128)(2,1)} %shard_map.64), slice={[4:7], [0:2], [0:12], [0:12], [0:128]} | slice | bytes 442368 | tf_op jit(solution)/shard_map/slice | solution.py:385
  60.5 1.0 %slice_bitcast_fusion = bf16[4,2,12,12,128]{4,2,3,1,0:T(8,128)(2,1)S(1)} fusion(bf16[7,2,12,16,128]{4,3,2,1,0:T(8,128)(2,1)} %shard_map.64), kind=kLoop, calls=%fused_computation.1 | loop fusion | bytes 589824 | tf_op jit(solution)/shard_map/transpose | solution.py:384
  61.5 0.1 copy.7
  61.6 0.1 pad_maximum_fusion
  61.7 1.3 %copy.8 = bf16[7,2,12,12,128]{4,1,3,2,0:T(2,128)(2,1)} copy(bf16[7,2,12,12,128]{4,2,3,1,0:T(8,128)(2,1)S(1)} %pad_maximum_fusion) | data formatting | bytes 1032192 | tf_op jit(solution)/shard_map/concatenate | solution.py:385
